TPU v7x, 32 devices: a whole 2x2x4 slice. The times are simulated.
32 devices in a mesh: dp: 2 (over x), expert: 16 (over z, y, core).
Axes of the slice: x: 2, y: 2, z: 4, core: 2. Of those that a mesh axis runs over, the one named last changes fastest.
Arguments:
- query_reps: bfloat16 [256, 2048], P('dp'), as said below
- code_reps: bfloat16 [256, 2048], P('expert'), as said below
- positives: int32 [256], P('dp'), may hold values from 0 to 255, as said below
- file_lengths: int32 [16, 2, 8], P('expert', 'dp'), may hold values from 1 to 64, 128 in all within a row
- residual: bfloat16 [16, 256, 2048], P('expert', 'dp'), may hold values from -6 to 6
- norm_gain: bfloat16 [2048], replicated, may hold values from 0.25 to 1.75
- expert_ids: int32 [16, 256, 2], P('expert', 'dp'), may hold values from 0 to 15, as said below
- gate_units: int32 [16, 256, 2], P('expert', 'dp'), may hold values from 16 to 191
- w_gate: bfloat16 [16, 2048, 768], P('expert', 'dp'), may hold values from -0.125 to 0.125
- w_up: bfloat16 [16, 2048, 768], P('expert', 'dp'), may hold values from -0.125 to 0.125
- w_down: bfloat16 [16, 2048, 768], P('expert', 'dp'), may hold values from -0.21875 to 0.21875
Outputs:
- token_grad: bfloat16 [16, 256, 2048], P('expert', 'dp')
Inputs may be any that keep to these rules, and one draw needn't show every extreme that they name: `positives`: each code is the positive of exactly one query. `query_reps`: entries have magnitude at most 4 / sqrt(2048). `code_reps`: entries have magnitude at most 4 / sqrt(2048). `file_lengths`: the 8 lengths of one shard add up to 128. `expert_ids`: each token names 2 different experts; the tokens of one shard name each expert at most 24 times, and for each index of dp some expert is named exactly 24 times by the tokens of every shard with that index.
All inputs are finite; a program needn't handle non-finite values.
Results may differ from a plain program's by a relative error of at most 0.009.
Values may be sent and summed in bfloat16 or wider, within the bound.
A program may use at most 64 MiB of HBM per device.

v0:
```python
import jax
import jax.numpy as jnp
from jax import lax
from jax.sharding import PartitionSpec as P

SCORE_SCALE = 20.0
GRAD_SCALE = 2560.0
EPSILON = 1e-06


def joined(value, axis, join):
    pieces = jax.tree.map(lambda part: lax.all_gather(part, axis), value)
    head = jax.tree.map(lambda part: part[0], pieces)
    tail = jax.tree.map(lambda part: part[1:], pieces)
    subtotal, _ = lax.scan(lambda subtotal, slab: (join(subtotal, slab), None), head, tail)
    return subtotal


def softmax_pair(first, second):
    row_top = jnp.maximum(first[0], second[0])
    return (
        row_top,
        first[1] * jnp.exp(first[0] - row_top) + second[1] * jnp.exp(second[0] - row_top),
    )


def expert_backward(normed_rows, cot_rows, gate_rows, weight_gate, weight_up, weight_down):
    gate_pre = jnp.dot(normed_rows, weight_gate, preferred_element_type=jnp.float32)
    up_pre = jnp.dot(normed_rows, weight_up, preferred_element_type=jnp.float32)
    back_hidden = gate_rows[:, None] * jnp.dot(
        cot_rows, weight_down, preferred_element_type=jnp.float32
    )
    sigmoid_gate = jax.nn.sigmoid(gate_pre)
    grad_gate = (
        back_hidden * up_pre * sigmoid_gate * (1.0 + gate_pre * (1.0 - sigmoid_gate))
    ).astype(jnp.bfloat16)
    grad_up = (back_hidden * gate_pre * sigmoid_gate).astype(jnp.bfloat16)
    contract = (((1,), (1,)), ((), ()))
    input_grad = lax.dot_general(
        grad_gate, weight_gate, contract, preferred_element_type=jnp.float32
    )
    input_grad = input_grad + lax.dot_general(
        grad_up, weight_up, contract, preferred_element_type=jnp.float32
    )
    return input_grad.astype(jnp.bfloat16)


def per_device(
    query_reps,
    code_reps,
    positives,
    file_lengths,
    residual,
    norm_gain,
    expert_ids,
    gate_units,
    w_gate,
    w_up,
    w_down,
):
    owners = lax.axis_size("expert")
    columns = code_reps.shape[0]
    file_count = file_lengths.shape[2]
    tokens = residual.shape[1]
    model_width = residual.shape[2]
    pick_count = expert_ids.shape[2]
    capacity = 3 * tokens * pick_count // (2 * owners)
    scores = jnp.dot(query_reps, code_reps.T, preferred_element_type=jnp.float32) * SCORE_SCALE
    local_top = jnp.max(scores, axis=1)
    local_total = jnp.sum(jnp.exp(scores - local_top[:, None]), axis=1)
    row_top, row_total = joined((local_top, local_total), "expert", softmax_pair)
    probabilities = jnp.exp(scores - row_top[:, None]) / row_total[:, None]
    column_ids = lax.axis_index("expert") * columns + jnp.arange(columns, dtype=jnp.int32)
    onehot = (positives[:, None] == column_ids[None, :]).astype(jnp.float32)
    weights = (GRAD_SCALE * (probabilities - onehot)).astype(jnp.bfloat16)
    code_grad = lax.psum_scatter(
        lax.dot_general(
            weights, query_reps, (((0,), (0,)), ((), ())), preferred_element_type=jnp.float32
        ),
        "dp",
        scatter_dimension=0,
        tiled=True,
    )
    lengths = file_lengths[0, 0]
    file_cot = (code_grad / lengths[:, None].astype(jnp.float32)).astype(jnp.bfloat16)
    file_ends = jnp.cumsum(lengths)
    position = jnp.arange(tokens, dtype=jnp.int32)
    segment = jnp.sum((position[:, None] >= file_ends[None, :]).astype(jnp.int32), axis=1)
    member = (segment[:, None] == jnp.arange(file_count, dtype=jnp.int32)[None, :]).astype(
        jnp.bfloat16
    )
    token_cot = jnp.dot(member, file_cot, preferred_element_type=jnp.float32).astype(jnp.bfloat16)
    stream = residual[0].astype(jnp.float32)
    root_inverse = lax.rsqrt(jnp.mean(stream * stream, axis=-1, keepdims=True) + EPSILON)
    norm_scale = norm_gain.astype(jnp.float32)
    normed = (stream * root_inverse * norm_scale).astype(jnp.bfloat16)
    chosen = expert_ids[0].reshape(-1)
    gate_values = gate_units[0].reshape(-1)
    assign_count = chosen.shape[0]
    expert_table = (chosen[:, None] == jnp.arange(owners, dtype=jnp.int32)[None, :]).astype(
        jnp.int32
    )
    earlier = jnp.cumsum(expert_table, axis=0) - expert_table
    slot_rank = jnp.sum(earlier * expert_table, axis=1)
    slot_index = chosen * capacity + slot_rank
    source = (
        jnp.full((owners * capacity,), assign_count, jnp.int32)
        .at[slot_index]
        .set(jnp.arange(assign_count, dtype=jnp.int32))
    )
    filled = source < assign_count
    token_of = jnp.where(filled, source // pick_count, tokens)
    gate_pad = jnp.concatenate(
        [gate_values.astype(jnp.float32) / 256.0, jnp.zeros((1,), jnp.float32)]
    )
    send_gate = gate_pad[source].astype(jnp.bfloat16).reshape(owners, capacity)
    normed_pad = jnp.concatenate([normed, jnp.zeros((1, model_width), jnp.bfloat16)])
    send_rows = normed_pad[token_of].reshape(owners, capacity, model_width)
    gathered = (
        lax.all_gather(w_gate, "dp", axis=1, tiled=True),
        lax.all_gather(w_up, "dp", axis=1, tiled=True),
        lax.all_gather(w_down, "dp", axis=1, tiled=True),
    )
    weight_gate = gathered[0][0]
    weight_up = gathered[1][0]
    weight_down = gathered[2][0]
    cot_pad = jnp.concatenate([token_cot, jnp.zeros((1, model_width), jnp.bfloat16)])
    send_cot = cot_pad[token_of].reshape(owners, capacity, model_width)
    row_block = lax.all_to_all(send_rows, "expert", split_axis=0, concat_axis=0, tiled=True)
    cot_block = lax.all_to_all(send_cot, "expert", split_axis=0, concat_axis=0, tiled=True)
    gate_rows = lax.all_to_all(send_gate, "expert", split_axis=0, concat_axis=0, tiled=True)
    senders = gate_rows.shape[0]
    items = gate_rows.shape[1]
    input_grad = expert_backward(
        row_block.reshape(-1, model_width),
        cot_block.reshape(-1, model_width),
        gate_rows.reshape(-1).astype(jnp.float32),
        weight_gate,
        weight_up,
        weight_down,
    )
    result = input_grad.reshape(senders, items, model_width)
    returned = lax.all_to_all(result, "expert", split_axis=0, concat_axis=0, tiled=True)
    per_pick = returned.reshape(owners * capacity, model_width)[slot_index].astype(jnp.float32)
    normed_grad = jnp.sum(per_pick.reshape(tokens, pick_count, model_width), axis=1)
    scaled = norm_scale * normed_grad
    correction = jnp.mean(scaled * stream, axis=-1, keepdims=True)
    token_grad = (
        token_cot.astype(jnp.float32)
        + root_inverse * scaled
        - stream * root_inverse**3 * correction
    )
    return token_grad.astype(jnp.bfloat16)[None]


def solution(mesh):
    return jax.shard_map(
        per_device,
        mesh=mesh,
        in_specs=(
            P("dp", None),
            P("expert", None),
            P("dp"),
            P("expert", "dp", None),
            P("expert", "dp", None),
            P(),
            P("expert", "dp", None),
            P("expert", "dp", None),
            P("expert", "dp", None),
            P("expert", "dp", None),
            P("expert", "dp", None),
        ),
        out_specs=P("expert", "dp", None),
        check_vma=False,
    )
```

profile of v0, /device:TPU:13, one launch (start us, length us, event | category | flops | bytes accessed | tf_op | source)
XLA Modules:
  0.0 272.9 jit_solution(16945070797731557296)
XLA Ops:
  6.5 1.0 copy-done
  7.6 1.1 fusion.65
  8.7 15.5 %all-gather.3 = f32[16,1,128]{2,1,0:T(1,128)S(1)} all-gather(f32[1,1,128]{2,1,0:T(1,128)S(1)} %bitcast.108), channel_id=3, replica_groups=mesh['dp'=2,'expert'=16] {'expert'}, dimensions={0}, use_global_device_ids=true | all-gather | bytes 8704 | tf_op jit(solution)/shard_map/all_gather | solution.py:12
  24.2 21.2 %all-gather.2 = f32[16,1,128]{2,1,0:T(1,128)S(1)} all-gather(f32[1,1,128]{2,1,0:T(1,128)S(1)} %bitcast.104), channel_id=2, replica_groups=mesh['dp'=2,'expert'=16] {'expert'}, dimensions={0}, use_global_device_ids=true | all-gather | bytes 8704 | tf_op jit(solution)/shard_map/all_gather | solution.py:12
  45.4 0.6 while.12
  46.1 1.6 fusion.50
  47.7 0.7 all-gather.12.cloned.1.call-update
  48.9 0.6 reduce-window.19
  50.4 1.4 scatter_custom_fusion
  51.8 2.8 %gather_fusion = bf16[384]{0:T(512)(128)(2,1)S(1)} fusion(bf16[257]{0:T(512)(128)(2,1)S(1)} %pad_maximum_fusion, s32[1024]{0:T(1024)S(1)} %pad_clamp_fusion.2), kind=kCustom, calls=%fused_computation | custom fusion | bytes 3072 | tf_op jit(solution)/shard_map/gather | solution.py:116
  54.6 0.7 convert_element_type.124
  55.3 6.1 %all-to-all-start = ((bf16[16,1,24]{2,1,0:T(2,128)(2,1)}), bf16[16,1,24]{2,1,0:T(2,128)(2,1)S(1)}, u32[]{:S(2)}, u32[]{:S(2)}) async-start(bf16[16,1,24]{2,1,0:T(2,128)(2,1)} %convert_element_type.124), calls=%async_computation.1 | async-start | bytes 16384 | tf_op jit(solution)/shard_map/all_to_all | solution.py:131
  62.0 3.1 %gather_fusion.2 = bf16[384,2048]{1,0:T(8,128)(2,1)} fusion(bf16[129,2048]{1,0:T(8,128)(2,1)S(1)} %concatenate.11, s32[1024]{0:T(1024)S(1)} %pad_clamp_fusion.1), kind=kCustom, calls=%fused_computation.2 | custom fusion | bytes 3147264 | tf_op jit(solution)/shard_map/gather | solution.py:118
  65.3 6.9 %all-to-all-start.2 = ((bf16[16,24,2048]{2,1,0:T(8,128)(2,1)}), bf16[16,24,2048]{2,1,0:T(8,128)(2,1)}, u32[]{:S(2)}, u32[]{:S(2)}) async-start(bf16[16,24,2048]{2,1,0:T(8,128)(2,1)} %bitcast.17), calls=%async_computation.3 | async-start | bytes 3145728 | tf_op jit(solution)/shard_map/all_to_all | solution.py:129
  72.2 0.7 all-gather.8.cloned.1.call-update
  73.2 1.2 convolution_convert_fusion
  74.5 3.1 %gather_fusion.1 = bf16[384,2048]{1,0:T(8,128)(2,1)} fusion(bf16[129,2048]{1,0:T(8,128)(2,1)S(1)} %concatenate.10, s32[1024]{0:T(1024)S(1)} %pad_clamp_fusion.1), kind=kCustom, calls=%fused_computation.1 | custom fusion | bytes 3147264 | tf_op jit(solution)/shard_map/gather | solution.py:128
  77.6 30.9 %all-to-all-done.2 = bf16[16,24,2048]{2,1,0:T(8,128)(2,1)} async-done(((bf16[16,24,2048]{2,1,0:T(8,128)(2,1)}), bf16[16,24,2048]{2,1,0:T(8,128)(2,1)}, u32[]{:S(2)}, u32[]{:S(2)}) %all-to-all-start.2) | async-done | bytes 1572896 | tf_op jit(solution)/shard_map/all_to_all | solution.py:129
  108.5 4.9 %all-to-all-start.1 = ((bf16[16,24,2048]{2,1,0:T(8,128)(2,1)}), bf16[16,24,2048]{2,1,0:T(8,128)(2,1)S(1)}, u32[]{:S(2)}, u32[]{:S(2)}) async-start(bf16[16,24,2048]{2,1,0:T(8,128)(2,1)} %bitcast.13), calls=%async_computation.2 | async-start | bytes 3145728 | tf_op jit(solution)/shard_map/all_to_all | solution.py:130
  113.6 0.3 all-gather.10.cloned.1.call-update
  114.1 5.4 %fusion.7 = f32[384,768]{1,0:T(8,128)} fusion(bf16[384,2048]{1,0:T(8,128)(2,1)} %bitcast.18, bf16[1,2048,768]{2,1,0:T(8,128)(2,1)} %all-gather.12.cloned.1.call-done), kind=kOutput, calls=%fused_computation.14 | convolution fusion | flops 1207959552 | bytes 5898240 | tf_op jit(solution)/shard_map/dot_general | solution.py:28
  119.5 32.1 %all-gather.8.cloned.1.call-done = bf16[1,2048,768]{2,1,0:T(8,128)(2,1)} async-done(((bf16[1,1024,768]{2,1,0:T(8,128)(2,1)}), bf16[1,2048,768]{2,1,0:T(8,128)(2,1)}) %all-gather.8.cloned.1.call-update) | async-done | bytes 3145744 | tf_op jit(solution)/shard_map/all_gather | solution.py:122
  151.5 4.3 %fusion.17 = f32[384,768]{1,0:T(8,128)} fusion(bf16[384,2048]{1,0:T(8,128)(2,1)S(1)} %bitcast.100, bf16[1,2048,768]{2,1,0:T(8,128)(2,1)} %all-gather.8.cloned.1.call-done, f32[384]{0:T(512)S(1)} %reshape.167), kind=kOutput, calls=%fused_computation.28 | convolution fusion | flops 1208254464 | bytes 5899776 | tf_op jit(solution)/shard_map/dot_general | solution.py:30
  155.8 42.1 %all-gather.10.cloned.1.call-done = bf16[1,2048,768]{2,1,0:T(8,128)(2,1)} async-done(((bf16[1,1024,768]{2,1,0:T(8,128)(2,1)}), bf16[1,2048,768]{2,1,0:T(8,128)(2,1)}) %all-gather.10.cloned.1.call-update) | async-done | bytes 3145744 | tf_op jit(solution)/shard_map/all_gather | solution.py:121
  197.9 8.8 %fusion.5 = f32[384,2048]{1,0:T(8,128)} fusion(bf16[1,2048,768]{2,1,0:T(8,128)(2,1)} %all-gather.12.cloned.1.call-done, f32[384,768]{1,0:T(8,128)} %fusion.17, bf16[384,2048]{1,0:T(8,128)(2,1)} %bitcast.18, bf16[1,2048,768]{2,1,0:T(8,128)(2,1)} %all-gather.10.cloned.1.call-done, f32[384,768]{1,0:T(8,128)} %fusion.7), kind=kOutput, calls=%fused_computation.12 | convolution fusion | flops 2418868224 | bytes 13369344 | tf_op jit(solution)/shard_map/dot_general | solution.py:39
  206.7 5.8 %add_convert_fusion = bf16[384,2048]{1,0:T(8,128)(2,1)} fusion(f32[384,2048]{1,0:T(8,128)} %fusion.5, bf16[1,2048,768]{2,1,0:T(8,128)(2,1)} %all-gather.10.cloned.1.call-done, f32[384,768]{1,0:T(8,128)} %fusion.17, f32[384,768]{1,0:T(8,128)S(1)} %copy-done.6), kind=kOutput, calls=%fused_computation.22 | convolution fusion | flops 1211301888 | bytes 10223616 | tf_op jit(solution)/shard_map/dot_general | solution.py:42
  212.5 6.4 %all-to-all-start.3 = ((bf16[16,24,2048]{2,1,0:T(8,128)(2,1)}), bf16[16,24,2048]{2,1,0:T(8,128)(2,1)S(1)}, u32[]{:S(2)}, u32[]{:S(2)}) async-start(bf16[16,24,2048]{2,1,0:T(8,128)(2,1)} %bitcast.101), calls=%async_computation.4 | async-start | bytes 3145728 | tf_op jit(solution)/shard_map/all_to_all | solution.py:143
  218.8 36.2 %all-to-all-done.3 = bf16[16,24,2048]{2,1,0:T(8,128)(2,1)S(1)} async-done(((bf16[16,24,2048]{2,1,0:T(8,128)(2,1)}), bf16[16,24,2048]{2,1,0:T(8,128)(2,1)S(1)}, u32[]{:S(2)}, u32[]{:S(2)}) %all-to-all-start.3) | async-done | bytes 1572896 | tf_op jit(solution)/shard_map/all_to_all | solution.py:143
  255.0 2.3 gather_fusion.3
  257.4 3.4 %reshape.168 = f32[128,2,2048]{2,1,0:T(2,128)} reshape(bf16[256,2048]{1,0:T(8,128)(2,1)} %gather_fusion.3) | data formatting | bytes 3145728 | tf_op jit(solution)/shard_map/convert_element_type | solution.py:144
  260.8 4.1 %reduce_sum.61 = f32[128,2048]{1,0:T(8,128)S(1)} reduce(f32[128,2,2048]{2,1,0:T(2,128)} %reshape.168, f32[]{:T(128)} %constant.23.clone.1), dimensions={1}, to_apply=%region_12.13 | reduce | flops 262144 | bytes 3145732 | tf_op jit(solution)/shard_map/reduce_sum | solution.py:145
  265.1 1.2 fusion.43
  (79 shorter events, 3.5 us)
Async XLA Ops:
  6.5 1.0 copy-start
  6.5 66.7 %reduce-scatter.2.cloned.1.call-start = ((), (), s32[]{:S(2)}) async-start(), calls=%async_computation.5 | async-start | bytes 196608 | tf_op jit(solution)/shard_map/reduce_scatter | solution.py:76
  7.6 40.9 %copy-start.2 = (s32[1,128,2]{1,2,0:T(2,128)S(1)}, s32[1,128,2]{1,2,0:T(2,128)}, u32[]{:S(2)}) copy-start(s32[1,128,2]{1,2,0:T(2,128)} %param.19) | copy-start | bytes 3076
  8.7 41.3 %copy-start.4 = (s32[1,128,2]{1,2,0:T(2,128)S(1)}, s32[1,128,2]{1,2,0:T(2,128)}, u32[]{:S(2)}) copy-start(s32[1,128,2]{1,2,0:T(2,128)} %param.20) | copy-start | bytes 3076
  47.7 13.8 %copy-start.3 = (bf16[2048]{0:T(1024)(128)(2,1)S(1)}, bf16[2048]{0:T(1024)(128)(2,1)}, u32[]{:S(2)}) copy-start(bf16[2048]{0:T(1024)(128)(2,1)} %param.18) | copy-start | bytes 12292
  47.7 13.8 %copy-start.1 = (bf16[1,128,2048]{2,1,0:T(8,128)(2,1)S(1)}, bf16[1,128,2048]{2,1,0:T(8,128)(2,1)}, u32[]{:S(2)}) copy-start(bf16[1,128,2048]{2,1,0:T(8,128)(2,1)} %param.17) | copy-start | bytes 1572868
  47.7 66.4 %all-gather.12.cloned.1.call-start = ((), (), s32[]{:S(2)}) async-start(), calls=%async_computation.8 | async-start | bytes 4718592 | tf_op jit(solution)/shard_map/all_gather | solution.py:120
  55.3 10.0 %all-to-all-start = ((bf16[16,1,24]{2,1,0:T(2,128)(2,1)}), bf16[16,1,24]{2,1,0:T(2,128)(2,1)S(1)}, u32[]{:S(2)}, u32[]{:S(2)}) async-start(bf16[16,1,24]{2,1,0:T(2,128)(2,1)} %convert_element_type.124), calls=%async_computation.1 | async-start | bytes 16384 | tf_op jit(solution)/shard_map/all_to_all | solution.py:131
  65.3 43.2 %all-to-all-start.2 = ((bf16[16,24,2048]{2,1,0:T(8,128)(2,1)}), bf16[16,24,2048]{2,1,0:T(8,128)(2,1)}, u32[]{:S(2)}, u32[]{:S(2)}) async-start(bf16[16,24,2048]{2,1,0:T(8,128)(2,1)} %bitcast.17), calls=%async_computation.3 | async-start | bytes 3145728 | tf_op jit(solution)/shard_map/all_to_all | solution.py:129
  72.2 0.7 copy-start.5
  72.2 79.4 %all-gather.8.cloned.1.call-start = ((), (), s32[]{:S(2)}) async-start(), calls=%async_computation.6 | async-start | bytes 4718592 | tf_op jit(solution)/shard_map/all_gather | solution.py:122
  108.5 43.1 %all-to-all-start.1 = ((bf16[16,24,2048]{2,1,0:T(8,128)(2,1)}), bf16[16,24,2048]{2,1,0:T(8,128)(2,1)S(1)}, u32[]{:S(2)}, u32[]{:S(2)}) async-start(bf16[16,24,2048]{2,1,0:T(8,128)(2,1)} %bitcast.13), calls=%async_computation.2 | async-start | bytes 3145728 | tf_op jit(solution)/shard_map/all_to_all | solution.py:130
  113.4 84.5 %all-gather.10.cloned.1.call-start = ((), (), s32[]{:S(2)}) async-start(), calls=%async_computation.7 | async-start | bytes 4718592 | tf_op jit(solution)/shard_map/all_gather | solution.py:121
  155.8 50.8 %copy-start.6 = (f32[384,768]{1,0:T(8,128)S(1)}, f32[384,768]{1,0:T(8,128)}, u32[]{:S(2)}) copy-start(f32[384,768]{1,0:T(8,128)} %fusion.7) | copy-start | bytes 3538948
  212.5 42.6 %all-to-all-start.3 = ((bf16[16,24,2048]{2,1,0:T(8,128)(2,1)}), bf16[16,24,2048]{2,1,0:T(8,128)(2,1)S(1)}, u32[]{:S(2)}, u32[]{:S(2)}) async-start(bf16[16,24,2048]{2,1,0:T(8,128)(2,1)} %bitcast.101), calls=%async_computation.4 | async-start | bytes 3145728 | tf_op jit(solution)/shard_map/all_to_all | solution.py:143
Sparse Core Ops, SparseCore 0:
  47.8 10.6 reduce-scatter.1
  60.0 44.9 all-gather.11
  106.6 44.9 all-gather.7
  152.9 44.9 all-gather.9
where the time goes:
time: 273 us
  waiting for transfers between devices  143 us (52%)
  blocking collectives  36.7 us (13%)
  matrix products  28 us (10%)
  starting transfers between devices  24.6 us (9%)
  local copies, waits for them, and re-layouts  19.2 us (7%)
  between operations  13.4 us (5%)
  other arithmetic  7.52 us (3%)
    all_gather x1, waiting for transfers between devices, per_device(): lax.all_gather(w_up, 'dp', axis=1, tiled=True)  42.1 us
    all_gather x2, blocking collectives, joined(): pieces = jax.tree.map(lambda part: lax.all_gather(part, axis), value)  36.7 us
    all_to_all x1, waiting for transfers between devices, per_device(): lax.all_to_all(result, 'expert', split_axis=0, concat_axis=0, tiled=True)  36.2 us
    all_gather x1, waiting for transfers between devices, per_device(): lax.all_gather(w_down, 'dp', axis=1, tiled=True)  32.1 us
    all_to_all x1, waiting for transfers between devices, per_device(): lax.all_to_all(send_rows, 'expert', split_axis=0, concat_axis=0, tiled=True)  30.9 us
    dot_general x1, matrix products, expert_backward(): lax.dot_general(grad_gate, weight_gate, contract, preferred_element_type=...  8.75 us
    all_to_all x1, starting transfers between devices, per_device(): lax.all_to_all(send_rows, 'expert', split_axis=0, concat_axis=0, tiled=True)  6.87 us
    all_to_all x1, starting transfers between devices, per_device(): lax.all_to_all(result, 'expert', split_axis=0, concat_axis=0, tiled=True)  6.38 us
  transfers between devices with their start and end apart: 8, of which 5 were waited for; matrix products, arithmetic and copies ran while one was open for 9% of the time, Pallas kernels for 0%

commit v1 on v0

--- a/solution.py
+++ b/solution.py
@@ -1,6 +1,10 @@
+import functools
+
 import jax
 import jax.numpy as jnp
 from jax import lax
+from jax.experimental import pallas as pl
+from jax.experimental.pallas import tpu as pltpu
 from jax.sharding import PartitionSpec as P
 
 SCORE_SCALE = 20.0
@@ -45,7 +49,7 @@
     return input_grad.astype(jnp.bfloat16)
 
 
-def per_device(
+def collective_plan(
     query_reps,
     code_reps,
     positives,
@@ -153,9 +157,429 @@
     return token_grad.astype(jnp.bfloat16)[None]
 
 
+MESH = pl.DeviceIdType.MESH
+CONTRACT_LAST = (((1,), (1,)), ((), ()))
+
+
+def matmul(left, right):
+    return jnp.dot(left, right, preferred_element_type=jnp.float32)
+
+
+def matmul_t(left, right):
+    return lax.dot_general(left, right, CONTRACT_LAST, preferred_element_type=jnp.float32)
+
+
+def iota(shape, axis):
+    return lax.broadcasted_iota(jnp.int32, shape, axis)
+
+
+def fused_kernel(
+    owners,
+    lengths_ref,
+    query_ref,
+    code_ref,
+    positive_ref,
+    residual_ref,
+    gain_ref,
+    ids_ref,
+    units_ref,
+    gate_hbm,
+    up_hbm,
+    down_hbm,
+    out_ref,
+    query_all,
+    code_all,
+    positive_all,
+    gate_all,
+    up_all,
+    down_own,
+    rows_out,
+    rows_in,
+    meta_out,
+    meta_in,
+    back_out,
+    back_in,
+    back_total,
+    rows_expert,
+    hidden_back,
+    grad_hidden,
+    grads_out,
+    grads_in,
+    combine,
+    local_sem,
+    pair_send,
+    pair_recv,
+    code_send,
+    code_recv,
+    rows_send,
+    rows_recv,
+    meta_send,
+    meta_recv,
+    grads_send,
+    grads_recv,
+):
+    f32, bf16 = jnp.float32, jnp.bfloat16
+    shard = lax.axis_index("dp")
+    me = lax.axis_index("expert")
+    other = 1 - shard
+    tokens, width = residual_ref.shape
+    half = width // 2
+    columns = code_ref.shape[0]
+    file_count = columns // 2
+    files = columns * owners
+    slots = meta_in.shape[1]
+    block = 2 * slots
+    ff = gate_all.shape[2]
+
+    def partner(step):
+        return lax.rem(me + step, owners)
+
+    def pair_copy(index, source, target):
+        return pltpu.make_async_remote_copy(
+            src_ref=source,
+            dst_ref=target,
+            send_sem=pair_send.at[index],
+            recv_sem=pair_recv.at[index],
+            device_id=(other, me),
+            device_id_type=MESH,
+        )
+
+    def group_copy(step, source, target, send, recv):
+        return pltpu.make_async_remote_copy(
+            src_ref=source,
+            dst_ref=target,
+            send_sem=send.at[step],
+            recv_sem=recv.at[step],
+            device_id=(shard, partner(step)),
+            device_id_type=MESH,
+        )
+
+    def code_copy(step):
+        return group_copy(step, code_ref, code_all.at[me], code_send, code_recv)
+
+    def rows_copy(step):
+        return group_copy(step, rows_out.at[partner(step)], rows_in.at[me], rows_send, rows_recv)
+
+    def meta_copy(step):
+        return group_copy(step, meta_out.at[partner(step)], meta_in.at[me], meta_send, meta_recv)
+
+    def grads_copy(step):
+        return group_copy(
+            step, grads_out.at[partner(step)], grads_in.at[me], grads_send, grads_recv
+        )
+
+    def each_partner(action):
+        def body(step, carry):
+            action(step)
+            return carry
+
+        lax.fori_loop(1, owners, body, 0)
+
+    barrier = pltpu.get_barrier_semaphore()
+    pl.semaphore_signal(barrier, inc=1, device_id=(other, me), device_id_type=MESH)
+    each_partner(
+        lambda step: pl.semaphore_signal(
+            barrier, inc=1, device_id=(shard, partner(step)), device_id_type=MESH
+        )
+    )
+    local_down = pltpu.make_async_copy(down_hbm, down_own, local_sem.at[0])
+    local_gate = pltpu.make_async_copy(gate_hbm, gate_all.at[shard], local_sem.at[1])
+    local_up = pltpu.make_async_copy(up_hbm, up_all.at[shard], local_sem.at[2])
+    local_down.start()
+    local_gate.start()
+    local_up.start()
+    query_all[shard] = query_ref[...]
+    code_all[me] = code_ref[...]
+    positive_all[shard] = jnp.broadcast_to(positive_ref[...], (8, positive_ref.shape[1]))
+    pl.semaphore_wait(barrier, owners)
+
+    query_pair = pair_copy(0, query_ref, query_all.at[shard])
+    positive_pair = pair_copy(1, positive_all.at[shard], positive_all.at[shard])
+    gate_pair = pair_copy(2, gate_hbm, gate_all.at[shard])
+    up_pair = pair_copy(3, up_hbm, up_all.at[shard])
+    back_pair = pair_copy(4, back_out.at[other], back_in)
+    query_pair.start()
+    positive_pair.start()
+    each_partner(lambda step: code_copy(step).start())
+
+    stream = residual_ref[...].astype(f32)
+    root_inverse = lax.rsqrt(jnp.mean(stream * stream, axis=-1, keepdims=True) + EPSILON)
+    gain = gain_ref[...].astype(f32)
+    normed = (stream * root_inverse * gain).astype(bf16)
+    lane = iota((tokens, 128), 1)
+    ids = ids_ref[...]
+    units = units_ref[...].astype(f32)
+    first = (ids[:, 0:1] == lane).astype(f32)
+    second = (ids[:, 1:2] == lane).astype(f32)
+    taken = first + second
+    share = first * units[:, 0:1] + second * units[:, 1:2]
+    before = (iota((tokens, tokens), 1) < iota((tokens, tokens), 0)).astype(bf16)
+    rank = matmul(before, taken.astype(bf16))
+    spread_lane = iota((128, owners * block), 1)
+    spread = (spread_lane // block == iota((128, owners * block), 0)).astype(bf16)
+    wide_taken = matmul(taken.astype(bf16), spread)
+    wide_rank = matmul(rank.astype(bf16), spread)
+    wide_share = matmul(share.astype(bf16), spread)
+    place = iota((tokens, owners * block), 1) % block
+    slot_hit = jnp.where(
+        (wide_taken > 0.5) & (wide_rank == (place % slots).astype(f32)), 1.0, 0.0
+    )
+    low = jnp.where(place < slots, slot_hit, 0.0)
+    high = slot_hit - low
+    select = jnp.concatenate([low, high], axis=0)
+    weighted = select * jnp.concatenate([wide_share, wide_share], axis=0) * (1.0 / 256.0)
+    combine[...] = weighted.astype(bf16)
+    pick = select.T.astype(bf16)
+    stacked = jnp.concatenate([normed[:, :half], normed[:, half:]], axis=0)
+    for tile in range(0, half, 256):
+        rows = matmul(pick, stacked[:, tile : tile + 256]).astype(bf16)
+        rows_out[:, :, tile : tile + 256] = rows.reshape(owners, block, 256)
+
+    place_t = iota((tokens, 128), 0)
+    file_place = iota((tokens, files), 1)
+    token_row = iota((tokens, files), 0)
+    inverse = jnp.zeros((tokens, 1), f32)
+    member = jnp.zeros((tokens, 128), f32)
+    member_all = jnp.zeros((tokens, files), f32)
+    end = 0
+    for file in range(file_count):
+        length = lengths_ref[0, file]
+        start, end = end, end + length
+        inside = (place_t >= start) & (place_t < end)
+        member = jnp.where(inside & (lane == me * file_count + file), 1.0, member)
+        inside_all = (token_row >= start) & (token_row < end)
+        owned = (me * 2 + shard) * file_count + file
+        member_all = jnp.where(inside_all & (file_place == owned), 1.0, member_all)
+        length_row = jnp.zeros((tokens, 1), f32) + length.astype(f32)
+        row_id = iota((tokens, 1), 0)
+        inverse = jnp.where((row_id >= start) & (row_id < end), 1.0 / length_row, inverse)
+    spread_meta = (
+        iota((128, owners * slots), 1) // slots == iota((128, owners * slots), 0)
+    ).astype(bf16)
+    meta_taken = matmul(taken.astype(bf16), spread_meta)
+    meta_rank = matmul(rank.astype(bf16), spread_meta)
+    meta_slot = (iota((tokens, owners * slots), 1) % slots).astype(f32)
+    meta_hit = jnp.where((meta_taken > 0.5) & (meta_rank == meta_slot), 1.0, 0.0).T
+    meta_hit = meta_hit.astype(bf16)
+    slot_inverse = jnp.dot(
+        meta_hit.astype(f32),
+        jnp.broadcast_to(inverse, (tokens, 128)),
+        precision=lax.Precision.HIGHEST,
+        preferred_element_type=f32,
+    )
+    meta = matmul(meta_hit, member.astype(bf16)) * slot_inverse
+    meta_out[...] = meta.reshape(owners, slots, 128)
+
+    rows_in[me] = rows_out[me]
+    meta_in[me] = meta_out[me]
+    each_partner(lambda step: meta_copy(step).start())
+    each_partner(lambda step: rows_copy(step).start())
+    gate_pair.start()
+    up_pair.start()
+
+    query_pair.wait()
+    positive_pair.wait()
+    each_partner(lambda step: code_copy(step).wait())
+    queries = query_all[...].reshape(files, width)
+    codes = code_all[...].reshape(files, width)
+    scores = matmul_t(codes, queries) * SCORE_SCALE
+    top = jnp.max(scores, axis=0, keepdims=True)
+    exponent = jnp.exp(scores - top)
+    probabilities = exponent / jnp.sum(exponent, axis=0, keepdims=True)
+    positives = jnp.concatenate([positive_all[0, 0:1], positive_all[1, 0:1]], axis=1)
+    onehot = (iota((files, files), 0) == positives).astype(f32)
+    weights = (GRAD_SCALE * (probabilities - onehot)).astype(bf16)
+    own = pl.ds(pl.multiple_of(shard * half, half), half)
+    half_queries = query_all[:, :, own].reshape(files, half)
+    code_grad = matmul(weights, half_queries).astype(bf16)
+    local_down.wait()
+    for tile in range(0, ff, 256):
+        part = matmul(code_grad, down_own[:, tile : tile + 256])
+        part = part.reshape(owners, 2, file_count, 256)
+        for side in range(2):
+            back_out[side, :, tile : tile + 256] = part[:, side].reshape(
+                owners * file_count, 256
+            )
+    back_pair.start()
+    token_weights = matmul(member_all.astype(bf16), weights).astype(bf16)
+    token_cot = (matmul(token_weights, queries) * inverse).astype(bf16)
+
+    each_partner(lambda step: meta_copy(step).wait())
+    each_partner(lambda step: rows_copy(step).wait())
+    rows_f32 = rows_in[...].astype(f32)
+    for side in range(2):
+        rows_expert[side] = (
+            rows_f32[:, side * slots : (side + 1) * slots].reshape(owners * slots, half)
+        ).astype(bf16)
+    back_pair.wait()
+    back_total[...] = (back_out[shard] + back_in[...]).astype(bf16)
+    meta_rows = meta_in[...].reshape(owners * slots, 128)
+    chosen = jnp.where(meta_rows > 0.0, 1.0, 0.0).astype(bf16)
+    chosen_scale = jnp.sum(meta_rows, axis=1, keepdims=True)
+    for tile in range(0, ff, 256):
+        hidden_back[:, tile : tile + 256] = (
+            matmul(chosen[:, : owners * file_count], back_total[:, tile : tile + 256])
+            * chosen_scale
+        )
+    local_gate.wait()
+    local_up.wait()
+    gate_pair.wait()
+    up_pair.wait()
+
+    def hidden_tile(tile, carry):
+        where = pl.ds(pl.multiple_of(tile * 256, 256), 256)
+        gate_pre = matmul(rows_expert[0], gate_all[0, :, where]) + matmul(
+            rows_expert[1], gate_all[1, :, where]
+        )
+        up_pre = matmul(rows_expert[0], up_all[0, :, where]) + matmul(
+            rows_expert[1], up_all[1, :, where]
+        )
+        back_hidden = hidden_back[:, where]
+        sigmoid_gate = jax.nn.sigmoid(gate_pre)
+        grad_hidden[0, :, where] = (
+            back_hidden * up_pre * sigmoid_gate * (1.0 + gate_pre * (1.0 - sigmoid_gate))
+        ).astype(bf16)
+        grad_hidden[1, :, where] = (back_hidden * gate_pre * sigmoid_gate).astype(bf16)
+        return carry
+
+    lax.fori_loop(0, ff // 256, hidden_tile, 0)
+
+    def grad_tile(tile, carry):
+        where = pl.ds(pl.multiple_of(tile * 256, 256), 256)
+        sides = []
+        for side in range(2):
+            part = matmul_t(grad_hidden[0], gate_all[side, where, :]) + matmul_t(
+                grad_hidden[1], up_all[side, where, :]
+            )
+            sides.append(part.reshape(owners, slots, 256))
+        grads_out[:, :, where] = jnp.concatenate(sides, axis=1).astype(bf16)
+        return carry
+
+    lax.fori_loop(0, half // 256, grad_tile, 0)
+
+    grads_in[me] = grads_out[me]
+    each_partner(lambda step: grads_copy(step).start())
+    each_partner(lambda step: grads_copy(step).wait())
+
+    picked = grads_in[...].reshape(owners * block, half)
+    summed = matmul(combine[...], picked)
+    normed_grad = jnp.concatenate([summed[:tokens], summed[tokens:]], axis=1)
+    scaled = gain * normed_grad
+    correction = jnp.mean(scaled * stream, axis=-1, keepdims=True)
+    out_ref[...] = (
+        token_cot.astype(f32)
+        + root_inverse * scaled
+        - stream * (root_inverse * root_inverse * root_inverse) * correction
+    ).astype(bf16)
+
+
+def per_device(
+    mesh,
+    query_reps,
+    code_reps,
+    positives,
+    file_lengths,
+    residual,
+    norm_gain,
+    expert_ids,
+    gate_units,
+    w_gate,
+    w_up,
+    w_down,
+):
+    owners = mesh.shape["expert"]
+    columns, width = code_reps.shape
+    files = owners * columns
+    tokens = residual.shape[1]
+    picks = expert_ids.shape[2]
+    file_count = file_lengths.shape[2]
+    ff = w_gate.shape[2]
+    slots = 3 * tokens * picks // (2 * owners)
+    fits = (
+        mesh.shape["dp"] == 2
+        and picks == 2
+        and files <= 256
+        and tokens == 128
+        and owners * file_count <= 128
+        and slots % 8 == 0
+        and width % 512 == 0
+        and ff % 256 == 0
+    )
+    if not fits:
+        return collective_plan(
+            query_reps,
+            code_reps,
+            positives,
+            file_lengths,
+            residual,
+            norm_gain,
+            expert_ids,
+            gate_units,
+            w_gate,
+            w_up,
+            w_down,
+        )
+    half = width // 2
+    block = 2 * slots
+    bf16, f32 = jnp.bfloat16, jnp.float32
+    vmem = pl.BlockSpec(memory_space=pltpu.VMEM)
+    hbm = pl.BlockSpec(memory_space=pl.ANY)
+    dma = pltpu.SemaphoreType.DMA
+    result = pl.pallas_call(
+        functools.partial(fused_kernel, owners),
+        out_shape=jax.ShapeDtypeStruct((tokens, width), bf16),
+        in_specs=[pl.BlockSpec(memory_space=pltpu.SMEM)] + [vmem] * 7 + [hbm] * 3,
+        out_specs=vmem,
+        scratch_shapes=[
+            pltpu.VMEM((2, files // 2, width), bf16),
+            pltpu.VMEM((owners, columns, width), bf16),
+            pltpu.VMEM((2, 8, files // 2), jnp.int32),
+            pltpu.VMEM((2, half, ff), bf16),
+            pltpu.VMEM((2, half, ff), bf16),
+            pltpu.VMEM((half, ff), bf16),
+            pltpu.VMEM((owners, block, half), bf16),
+            pltpu.VMEM((owners, block, half), bf16),
+            pltpu.VMEM((owners, slots, 128), f32),
+            pltpu.VMEM((owners, slots, 128), f32),
+            pltpu.VMEM((2, files // 2, ff), f32),
+            pltpu.VMEM((files // 2, ff), f32),
+            pltpu.VMEM((files // 2, ff), bf16),
+            pltpu.VMEM((2, owners * slots, half), bf16),
+            pltpu.VMEM((owners * slots, ff), f32),
+            pltpu.VMEM((2, owners * slots, ff), bf16),
+            pltpu.VMEM((owners, block, half), bf16),
+            pltpu.VMEM((owners, block, half), bf16),
+            pltpu.VMEM((2 * tokens, owners * block), bf16),
+            dma((3,)),
+            dma((5,)),
+            dma((5,)),
+        ]
+        + [dma((owners,))] * 8,
+        compiler_params=pltpu.CompilerParams(
+            collective_id=0, has_side_effects=True, vmem_limit_bytes=52 * 1024 * 1024
+        ),
+        cost_estimate=pl.CostEstimate(
+            flops=5 * 10**9, bytes_accessed=6 * 10**6, transcendentals=10**6
+        ),
+    )(
+        file_lengths[0],
+        query_reps,
+        code_reps,
+        positives[None],
+        residual[0],
+        norm_gain[None],
+        expert_ids[0],
+        gate_units[0],
+        w_gate[0],
+        w_up[0],
+        w_down[0],
+    )
+    return result[None]
+
+
 def solution(mesh):
     return jax.shard_map(
-        per_device,
+        functools.partial(per_device, mesh),
         mesh=mesh,
         in_specs=(
             P("dp", None),

time: 273 us -> 145 us (0.53)
  waiting for transfers between devices: 143 us -> 0 us
  Pallas kernels: 0 us -> 138 us
  blocking collectives: 36.7 us -> 0 us
  matrix products: 28 us -> 0 us
  starting transfers between devices: 24.6 us -> 0 us
  between operations: 13.4 us -> 0.02 us
  local copies, waits for them, and re-layouts: 19.2 us -> 7.28 us
  other arithmetic: 7.52 us -> 0 us
    pallas_call x0 -> x1, Pallas kernels: none -> 138 us  [per_device(): pl.pallas_call(functools.partial(fused_kernel, owners), out_shape=jax.Sha...]
    all_gather x3 -> x0, waiting for transfers between devices: 74.2 us -> none  [the longest x1 42.1 us: per_device(): lax.all_gather(w_up, 'dp', axis=1, tiled=True)]
    all_to_all x4 -> x0, waiting for transfers between devices: 67.3 us -> none  [the longest x1 36.2 us: per_device(): lax.all_to_all(result, 'expert', split_axis=0, concat_axis=0, tiled=True)]
    all_gather x2 -> x0, blocking collectives: 36.7 us -> none  [joined(): pieces = jax.tree.map(lambda part: lax.all_gather(part, axis), value)]
    dot_general x7 -> x0, matrix products: 28 us -> none  [the longest x1 8.75 us: expert_backward(): lax.dot_general(grad_gate, weight_gate, contract, preferred_element_type=...]
    all_to_all x4 -> x0, starting transfers between devices: 24.3 us -> none  [the longest x1 6.87 us: per_device(): lax.all_to_all(send_rows, 'expert', split_axis=0, concat_axis=0, tiled=True)]
    gather x4 -> x0, local copies, waits for them, and re-layouts: 11.4 us -> none  [the longest x1 3.12 us: per_device(): send_cot = cot_pad[token_of].reshape(owners, capacity, model_width)]
    unnamed x17 -> x13, local copies, waits for them, and re-layouts: 1.19 us -> 6.59 us
  transfers between devices with their start and end apart: 8 -> 0, of which waited for: 5 -> 0; matrix products, arithmetic and copies ran while one was open for 9% -> 0% of each run, Pallas kernels for 0% -> 0%
where the time goes in v1:
time: 145 us
  Pallas kernels  138 us (95%)
  local copies, waits for them, and re-layouts  7.28 us (5%)
    pallas_call x1, Pallas kernels, per_device(): pl.pallas_call(functools.partial(fused_kernel, owners), out_shape=jax.Sha...  138 us
    unnamed x13, local copies, waits for them, and re-layouts  6.59 us

profile of v1, /device:TPU:13, one launch (start us, length us, event | category | flops | bytes accessed | tf_op | source)
XLA Modules:
  0.0 144.8 jit_solution(7384574360505335193)
XLA Ops:
  0.0 0.7 broadcast_in_dim.10.gain_ref
  0.7 0.8 copy.12
  1.5 0.8 copy.13
  2.3 0.0 copy-start
  2.3 1.0 copy-done
  3.3 0.0 copy-start.1
  3.3 1.0 copy-done.1
  4.3 0.0 copy-start.2
  4.3 0.8 copy-done.2
  5.2 0.0 copy-start.3
  5.2 0.7 copy-done.3
  5.8 0.0 copy-start.4
  5.8 0.7 copy-done.4
  6.5 137.5 %shard_map.109 = bf16[128,2048]{1,0:T(8,128)(2,1)S(1)} custom-call(s32[1,8]{1,0:T(1,128)S(1)} %bitcast.13, bf16[128,2048]{1,0:T(8,128)(2,1)S(1)} %copy-done, bf16[16,2048]{1,0:T(8,128)(2,1)S(1)} %copy-done.2, s32[1,128]{1,0:T(1,128)S(1)} %bitcast.14, bf16[128,2048]{1,0:T(8,128)(2,1)S(1)} %bitcast.12, bf16[1,2048]{1,0:T(2,128)(2,1)S(1)} %broadcast_in_dim.10.gain_ref, ...), custom_call_target="tpu_custom_call" | custom-call | flops 5000000000 | bytes 6000000 | tf_op jit(solution)/shard_map/pallas_call | solution.py:528
  144.0 0.8 copy.15
Async XLA Ops:
  2.3 1.0 copy-start
  3.3 1.0 copy-start.1
  4.3 0.8 copy-start.2
  5.2 0.7 copy-start.3
  5.8 0.7 copy-start.4
